TPU v7x, 512 devices: a whole 4x8x8 slice. The times are simulated.
512 devices in a mesh: depth: 8 (over z), tile: 64 (over y, x, core).
Axes of the slice: x: 4, y: 8, z: 8, core: 2. Of those that a mesh axis runs over, the one named last changes fastest.
Arguments:
- exit_grad: bfloat16 [256, 256, 2, 256], P('tile', 'depth'), may hold values from -6 to 6
- stored_waves: bfloat16 [16, 256, 256, 2, 256], P('depth', 'tile'), may hold values from -6 to 6
- object_slices: float32 [16, 448, 2, 16384], P('depth', None, None, 'tile'), may hold values from -4 to 4
- propagator_taps: float32 [2, 2, 31], replicated, may hold values from -0.75 to 0.75
- positions: int32 [256, 2], replicated, may hold values from 0 to 255, as said below
- counts: int32 [64], replicated, may hold values from 1 to 4, as said below
Outputs:
- object_grad: bfloat16 [16, 448, 2, 16384], P('depth', None, None, 'tile')
Inputs may be any that keep to these rules, and one draw needn't show every extreme that they name: Column 0 is a window's first row, 0 to 192; column 1 is a window's centre column within its tile, 0 to 255. Dead slots hold positions too. `counts`: some tile has exactly 4 live slots and some tile exactly 1.
All inputs are finite; a program needn't handle non-finite values.
Results may differ from a plain program's by a relative error of at most 0.034.
Values may be sent and summed in bfloat16 or wider, within the bound.
A program may use at most 64 MiB of HBM per device.

v0:
```python
import jax
import jax.numpy as jnp
from jax import lax
from jax.sharding import PartitionSpec as P


def sent_to_all(x, axis):
    devices = lax.axis_size(axis)
    return lax.all_to_all(jnp.broadcast_to(x[None], (devices, *x.shape)), axis, 0, 0, tiled=True)


def laid_out(parts, dim):
    parts = jnp.moveaxis(parts, 0, dim)
    dims = parts.shape
    return parts.reshape(*dims[:dim], dims[dim] * dims[dim + 1], *dims[dim + 2 :])


def gathered_copies(x, axis, dim):
    parts = sent_to_all(x, axis)
    return laid_out(parts, dim)


def extended(x, sides, width):
    for axis, dim in sides:
        devices, length = (lax.axis_size(axis), x.shape[dim])
        up = [(i, (i + 1) % devices) for i in range(devices)]
        down = [(j, i) for i, j in up]
        last = lax.slice_in_dim(x, length - width, length, axis=dim)
        leading = lax.slice_in_dim(x, 0, width, axis=dim)
        before = lax.ppermute(last, axis, up)
        after = lax.ppermute(leading, axis, down)
        x = jnp.concatenate([before, x, after], axis=dim)
    return x


def as_sent(x):

    def short(part):
        return part.astype(jnp.bfloat16) if part.dtype == jnp.float32 else part

    return jax.tree.map(short, x)


def shifted(block, axis, distance):
    devices = range(lax.axis_size(axis))
    route = [(i - distance, i) for i in devices if i - distance in devices]
    return lax.ppermute(block, axis, route)


def passed_along(value, axis, steps):
    count = lax.axis_size(axis)
    pairs = [(source, (source + steps) % count) for source in range(count)]
    return lax.ppermute(value, axis, pairs)


def band_blocks(propagator_taps, probe_side):
    tap_count = propagator_taps.shape[2]
    centre = tap_count // 2
    places = jnp.arange(probe_side, dtype=jnp.int32)
    offset = places[None, :] - places[:, None] + centre
    onehot = (
        offset.reshape(1, probe_side * probe_side)
        == jnp.arange(tap_count, dtype=jnp.int32)[:, None]
    ).astype(jnp.float32)
    flat_taps = jnp.dot(
        propagator_taps.reshape(4, tap_count),
        onehot,
        precision=lax.Precision.HIGHEST,
        preferred_element_type=jnp.float32,
    )
    matrices = flat_taps.reshape(2, 2, probe_side, probe_side)
    y_real, y_imag = (matrices[0, 0], matrices[0, 1])
    x_real, x_imag = (matrices[1, 0], matrices[1, 1])
    column_block = jnp.concatenate(
        [jnp.concatenate([x_real, -x_imag], 1), jnp.concatenate([x_imag, x_real], 1)], 0
    ).astype(jnp.bfloat16)
    row_block = jnp.concatenate([y_real.T, y_imag.T], 0).astype(jnp.bfloat16)
    return (column_block, row_block)


def propagate(wave_block, column_block, row_block):
    probe_side = wave_block.shape[1]
    flat_waves = wave_block.reshape(wave_block.shape[0], probe_side, 2 * probe_side)
    mixed = jnp.einsum(
        "mrc,cd->mrd", flat_waves, column_block, preferred_element_type=jnp.float32
    ).astype(jnp.bfloat16)
    stacked = jnp.einsum("ar,mrd->mad", row_block, mixed, preferred_element_type=jnp.float32)
    upper_half = stacked[:, :probe_side]
    lower_half = stacked[:, probe_side:]
    wave_real = upper_half[:, :, :probe_side] + lower_half[:, :, probe_side:]
    wave_imag = upper_half[:, :, probe_side:] - lower_half[:, :, :probe_side]
    return (wave_real, wave_imag)


def on_device(exit_grad, stored_waves, object_slices, propagator_taps, positions, counts):
    group_slices = stored_waves.shape[0]
    slot_cap = stored_waves.shape[1]
    probe_side = stored_waves.shape[2]
    half_side = probe_side // 2
    tile_cols = object_slices.shape[3]
    groups = lax.axis_size("depth")
    group_index = lax.axis_index("depth")
    tile_index = lax.axis_index("tile")
    column_block, row_block = band_blocks(propagator_taps, probe_side)
    exits = gathered_copies(exit_grad, "depth", 1)
    frames = extended(object_slices, (("tile", 3),), half_side)
    my_positions = lax.dynamic_slice_in_dim(positions, tile_index * slot_cap, slot_cap, 0)
    my_count = lax.dynamic_slice_in_dim(counts, tile_index, 1, 0)[0]
    block_size = 1
    block_total = slot_cap // block_size
    turn_count = block_total + groups - 1
    last_group = groups - 1

    def run_block(accumulator, incoming, block_index):
        first_slot = block_index * block_size
        chosen = lax.dynamic_slice_in_dim(my_positions, first_slot, block_size, 0)
        wave_block = incoming
        for layer_index in range(group_slices - 1, -1, -1):
            stored_block = lax.dynamic_slice_in_dim(
                stored_waves[layer_index], first_slot, block_size, 0
            )
            wave_real, wave_imag = propagate(wave_block, column_block, row_block)
            frame = frames[layer_index]
            layer_acc = accumulator[layer_index]
            row_start = chosen[0, 0]
            col_start = chosen[0, 1]
            weight = (first_slot + 0 < my_count).astype(jnp.float32)
            window = lax.dynamic_slice(
                frame, (row_start, 0, col_start), (probe_side, 2, probe_side)
            )
            stored_real = stored_block[0, :, 0].astype(jnp.float32)
            stored_imag = stored_block[0, :, 1].astype(jnp.float32)
            back_real = wave_real[0]
            back_imag = wave_imag[0]
            grad_real = stored_real * back_real + stored_imag * back_imag
            grad_imag = stored_real * back_imag - stored_imag * back_real
            term = jnp.stack([grad_real, grad_imag], 1) * weight
            region = lax.dynamic_slice(
                layer_acc, (row_start, 0, col_start), (probe_side, 2, probe_side)
            )
            layer_acc = lax.dynamic_update_slice(
                layer_acc, region + term, (row_start, 0, col_start)
            )
            obj_real = window[:, 0]
            obj_imag = window[:, 1]
            out_waves = [
                jnp.stack(
                    [
                        obj_real * back_real + obj_imag * back_imag,
                        obj_real * back_imag - obj_imag * back_real,
                    ],
                    1,
                ).astype(jnp.bfloat16)
            ]
            accumulator = lax.dynamic_update_index_in_dim(accumulator, layer_acc, layer_index, 0)
            wave_block = jnp.stack(out_waves)
        return (accumulator, wave_block)

    def spare_block(accumulator, incoming, block_index):
        return (accumulator, jnp.zeros_like(incoming))

    def relay_turn(turn_index, state_pair):
        accumulator, received = state_pair
        block_index = turn_index - (last_group - group_index)
        clipped = jnp.clip(block_index, 0, block_total - 1)
        fresh_waves = lax.dynamic_slice_in_dim(exits, clipped * block_size, block_size, 0)
        incoming = jnp.where(group_index == last_group, fresh_waves, received)
        active = (
            (block_index >= 0) & (block_index < block_total) & (clipped * block_size < my_count)
        )
        accumulator, outgoing = lax.cond(
            active, run_block, spare_block, accumulator, incoming, clipped
        )
        received = shifted(as_sent(outgoing), "depth", -1).astype(outgoing.dtype)
        return (accumulator, received)

    start_acc = jnp.zeros(frames.shape, jnp.float32)
    start_waves = jnp.zeros((block_size, probe_side, 2, probe_side), jnp.bfloat16)
    accumulator, received = lax.fori_loop(0, turn_count, relay_turn, (start_acc, start_waves))
    owned_part = accumulator[:, :, :, half_side : half_side + tile_cols]
    left_rim = accumulator[:, :, :, :half_side]
    right_rim = accumulator[:, :, :, tile_cols + half_side :]
    from_left = passed_along(right_rim.astype(jnp.bfloat16), "tile", 1).astype(right_rim.dtype)
    from_right = passed_along(left_rim.astype(jnp.bfloat16), "tile", -1).astype(left_rim.dtype)
    owned_part = owned_part.at[:, :, :, :half_side].add(from_left)
    owned_part = owned_part.at[:, :, :, tile_cols - half_side :].add(from_right)
    return owned_part.astype(jnp.bfloat16)


def solution(mesh):
    return jax.shard_map(
        on_device,
        mesh=mesh,
        in_specs=(
            P("tile", "depth", None, None),
            P("depth", "tile", None, None, None),
            P("depth", None, None, "tile"),
            P(),
            P(),
            P(),
        ),
        out_specs=P("depth", None, None, "tile"),
        check_vma=False,
    )
```

profile of v0, /device:TPU:9, one launch (start us, length us, event | category | flops | bytes accessed | tf_op | source)
XLA Modules:
  0.0 686.3 jit_solution(12351991143264197709)
XLA Ops:
  0.0 3.1 broadcast_in_dim.7
  3.1 10.0 %all-to-all-start = ((bf16[8,4,32,2,256]{4,3,2,1,0:T(2,128)(2,1)}), bf16[8,4,32,2,256]{4,3,2,1,0:T(2,128)(2,1)S(1)}, u32[]{:S(2)}, u32[]{:S(2)}) async-start(bf16[8,4,32,2,256]{4,3,2,1,0:T(2,128)(2,1)} %broadcast_in_dim.7), calls=%async_computation | async-start | bytes 2097152 | tf_op jit(solution)/shard_map/all_to_all | solution.py:9
  14.7 2.9 collective-permute-start.2
  18.6 3.0 collective-permute-start.1
  21.8 3.1 fusion.16
  27.3 2.7 copy.36
  30.0 6.1 copy.38
  41.5 2.5 copy.37
  44.0 2.5 copy.35
  46.4 4.2 pad_maximum_fusion.2
  50.9 2.1 copy.39
  53.0 2.6 broadcast_in_dim.6
  55.6 488.0 %while.22 = (s32[]{:T(128)}, f32[2,448,2,512]{1,3,2,0:T(8,128)}, bf16[1,256,2,256]{1,3,2,0:T(8,128)(2,1)S(1)}, s32[]{:T(128)}, s32[]{:T(128)}, /*index=5*/s32[4,...) while((s32[]{:T(128)}, f32[2,448,2,512]{1,3,2,0:T(8,128)}, ...), condition=%wide.region_3.4_spmd, body=%wide.region_0.3_spmd.sunk | while | flops 540672000 | bytes 66323136 | solution.py:179
  58.3 8.5 %collective-permute-done = bf16[1,256,2,256]{1,3,2,0:T(8,128)(2,1)S(1)} collective-permute-done((bf16[1,256,2,256]{1,3,2,0:T(8,128)(2,1)}, bf16[1,256,2,256]{1,3,2,0:T(8,128)(2,1)S(1)}, u32[]{:S(2)}, u32[]{:S(2)}) %collective-permute-start) | collective-permute-done | bytes 262176 | tf_op jit(solution)/shard_map/while/body/eval_jaxpr/ppermute | solution.py:47
  69.5 7.3 %collective-permute-done = bf16[1,256,2,256]{1,3,2,0:T(8,128)(2,1)S(1)} collective-permute-done((bf16[1,256,2,256]{1,3,2,0:T(8,128)(2,1)}, bf16[1,256,2,256]{1,3,2,0:T(8,128)(2,1)S(1)}, u32[]{:S(2)}, u32[]{:S(2)}) %collective-permute-start) | collective-permute-done | bytes 262176 | tf_op jit(solution)/shard_map/while/body/eval_jaxpr/ppermute | solution.py:47
  79.6 6.4 collective-permute-done
  88.7 7.9 %collective-permute-done = bf16[1,256,2,256]{1,3,2,0:T(8,128)(2,1)S(1)} collective-permute-done((bf16[1,256,2,256]{1,3,2,0:T(8,128)(2,1)}, bf16[1,256,2,256]{1,3,2,0:T(8,128)(2,1)S(1)}, u32[]{:S(2)}, u32[]{:S(2)}) %collective-permute-start) | collective-permute-done | bytes 262176 | tf_op jit(solution)/shard_map/while/body/eval_jaxpr/ppermute | solution.py:47
  99.3 6.4 collective-permute-done
  108.4 7.0 %collective-permute-done = bf16[1,256,2,256]{1,3,2,0:T(8,128)(2,1)S(1)} collective-permute-done((bf16[1,256,2,256]{1,3,2,0:T(8,128)(2,1)}, bf16[1,256,2,256]{1,3,2,0:T(8,128)(2,1)S(1)}, u32[]{:S(2)}, u32[]{:S(2)}) %collective-permute-start) | collective-permute-done | bytes 262176 | tf_op jit(solution)/shard_map/while/body/eval_jaxpr/ppermute | solution.py:47
  118.1 296.4 %collective-permute-done = bf16[1,256,2,256]{1,3,2,0:T(8,128)(2,1)S(1)} collective-permute-done((bf16[1,256,2,256]{1,3,2,0:T(8,128)(2,1)}, bf16[1,256,2,256]{1,3,2,0:T(8,128)(2,1)S(1)}, u32[]{:S(2)}, u32[]{:S(2)}) %collective-permute-start) | collective-permute-done | bytes 262176 | tf_op jit(solution)/shard_map/while/body/eval_jaxpr/ppermute | solution.py:47
  415.2 43.5 %conditional.2 = (f32[2,448,2,512]{1,3,2,0:T(8,128)}, bf16[1,256,2,256]{1,3,2,0:T(8,128)(2,1)}) conditional(s32[]{:T(128)} %convert_element_type.147, f32[2,448,2,512]{1,3,2,0:T(8,128)} %get-tuple-element.600, (f32[2,448,2,512]{1,3,2,0:T(8,128)}, s32[]{:T(128)}, s32[4,2]{0,1:T(2,128)S(1)}, bf16[2,4,256,2,256]{2,4,3,1,0:T(8,128)(2,1)}, pred[]{:T(512)}, ...), branch_computations={%region_1.1_spmd, %region_2.2_spmd} | conditional | flops 540672000 | bytes 65274212 | solution.py:171
  415.9 4.2 fusion.23
  427.7 1.7 convolution_bitcast_fusion.1
  430.5 1.6 convolution_bitcast_fusion
  433.1 1.9 slice.189
  436.7 8.4 %dynamic_update_slice.19 = f32[1,448,2,512]{1,3,2,0:T(8,128)S(1)} dynamic-update-slice(f32[1,448,2,512]{1,3,2,0:T(8,128)S(1)} %slice.189, f32[1,256,2,256]{1,3,2,0:T(8,128)S(1)} %fusion, s32[]{:T(128)} %constant.143.clone, s32[]{:T(128)S(6)} %select_n.57, s32[]{:T(128)} %constant.143.clone, s32[]{:T(128)S(6)} %select_n.58) | dynamic-update-slice | bytes 1048580 | tf_op jit(solution)/shard_map/while/body/eval_jaxpr/cond/branch_1_fun/dynamic_update_slice | solution.py:141
  445.1 1.6 constant_dynamic-update-slice_fusion.1
  446.7 1.8 slice.241
  448.8 8.4 %dynamic_update_slice.21 = f32[1,448,2,512]{1,3,2,0:T(8,128)S(1)} dynamic-update-slice(f32[1,448,2,512]{1,3,2,0:T(8,128)S(1)} %slice.241, f32[1,256,2,256]{1,3,2,0:T(8,128)S(1)} %fusion.1, s32[]{:T(128)} %constant.143.clone, s32[]{:T(128)S(6)} %select_n.57, s32[]{:T(128)} %constant.143.clone, s32[]{:T(128)S(6)} %select_n.58) | dynamic-update-slice | bytes 1048580 | tf_op jit(solution)/shard_map/while/body/eval_jaxpr/cond/branch_1_fun/dynamic_update_slice | solution.py:141
  460.0 13.3 %collective-permute-done = bf16[1,256,2,256]{1,3,2,0:T(8,128)(2,1)S(1)} collective-permute-done((bf16[1,256,2,256]{1,3,2,0:T(8,128)(2,1)}, bf16[1,256,2,256]{1,3,2,0:T(8,128)(2,1)S(1)}, u32[]{:S(2)}, u32[]{:S(2)}) %collective-permute-start) | collective-permute-done | bytes 262176 | tf_op jit(solution)/shard_map/while/body/eval_jaxpr/ppermute | solution.py:47
  474.0 44.7 %conditional.2 = (f32[2,448,2,512]{1,3,2,0:T(8,128)}, bf16[1,256,2,256]{1,3,2,0:T(8,128)(2,1)}) conditional(s32[]{:T(128)} %convert_element_type.147, f32[2,448,2,512]{1,3,2,0:T(8,128)} %get-tuple-element.600, (f32[2,448,2,512]{1,3,2,0:T(8,128)}, s32[]{:T(128)}, s32[4,2]{0,1:T(2,128)S(1)}, bf16[2,4,256,2,256]{2,4,3,1,0:T(8,128)(2,1)}, pred[]{:T(512)}, ...), branch_computations={%region_1.1_spmd, %region_2.2_spmd} | conditional | flops 540672000 | bytes 65274212 | solution.py:171
  474.7 4.2 fusion.23
  486.5 1.7 convolution_bitcast_fusion.1
  489.3 1.6 convolution_bitcast_fusion
  491.9 1.9 slice.189
  495.5 9.0 %dynamic_update_slice.19 = f32[1,448,2,512]{1,3,2,0:T(8,128)S(1)} dynamic-update-slice(f32[1,448,2,512]{1,3,2,0:T(8,128)S(1)} %slice.189, f32[1,256,2,256]{1,3,2,0:T(8,128)S(1)} %fusion, s32[]{:T(128)} %constant.143.clone, s32[]{:T(128)S(6)} %select_n.57, s32[]{:T(128)} %constant.143.clone, s32[]{:T(128)S(6)} %select_n.58) | dynamic-update-slice | bytes 1048580 | tf_op jit(solution)/shard_map/while/body/eval_jaxpr/cond/branch_1_fun/dynamic_update_slice | solution.py:141
  504.6 1.6 constant_dynamic-update-slice_fusion.1
  506.1 1.8 slice.241
  508.2 9.0 %dynamic_update_slice.21 = f32[1,448,2,512]{1,3,2,0:T(8,128)S(1)} dynamic-update-slice(f32[1,448,2,512]{1,3,2,0:T(8,128)S(1)} %slice.241, f32[1,256,2,256]{1,3,2,0:T(8,128)S(1)} %fusion.1, s32[]{:T(128)} %constant.143.clone, s32[]{:T(128)S(6)} %select_n.57, s32[]{:T(128)} %constant.143.clone, s32[]{:T(128)S(6)} %select_n.58) | dynamic-update-slice | bytes 1048580 | tf_op jit(solution)/shard_map/while/body/eval_jaxpr/cond/branch_1_fun/dynamic_update_slice | solution.py:141
  520.0 6.0 collective-permute-done
  528.8 6.0 collective-permute-done
  537.5 6.0 collective-permute-done
  543.5 7.2 %copy.40 = f32[2,448,2,512]{3,2,1,0:T(2,128)} copy(f32[2,448,2,512]{1,3,2,0:T(8,128)} %get-tuple-element.380) | data formatting | bytes 7340032 | tf_op jit(solution)/shard_map/while | solution.py:179
  550.7 3.3 convert.44
  554.7 119.4 %collective-permute-start.3 = (bf16[2,448,2,128]{3,2,1,0:T(2,128)(2,1)S(1)}, bf16[2,448,2,128]{3,2,1,0:T(2,128)(2,1)S(1)}, u32[]{:S(2)}, u32[]{:S(2)}) collective-permute-start(bf16[2,448,2,128]{3,2,1,0:T(2,128)(2,1)S(1)} %get-tuple-element.495), channel_id=1, source_target_pairs={{0,1},{1,2},{2,3},{3,4},{4,5},{5,6},{6,7},{7,8},{8,9},{9,10},{10,1... | collective-permute-start | bytes 1376264 | tf_op jit(solution)/shard_map/ppermute | solution.py:53
  674.1 1.9 collective-permute-start.4
  676.1 3.5 collective-permute-done.3
  680.3 3.6 collective-permute-done.4
  (122 shorter events, 60.0 us)
Async XLA Ops:
  0.0 21.8 %copy-start = (f32[2,2,31]{2,1,0:T(2,128)S(1)}, f32[2,2,31]{2,1,0:T(2,128)}, u32[]{:S(2)}) copy-start(f32[2,2,31]{2,1,0:T(2,128)} %param.17) | copy-start | bytes 1492
  0.0 13.1 %copy-start.7 = (f32[2,448,2,256]{3,2,1,0:T(2,128)S(1)}, f32[2,448,2,256]{3,2,1,0:T(2,128)}, u32[]{:S(2)}) copy-start(f32[2,448,2,256]{3,2,1,0:T(2,128)} %param.16) | copy-start | bytes 5505028
  3.1 47.6 %all-to-all-start = ((bf16[8,4,32,2,256]{4,3,2,1,0:T(2,128)(2,1)}), bf16[8,4,32,2,256]{4,3,2,1,0:T(2,128)(2,1)S(1)}, u32[]{:S(2)}, u32[]{:S(2)}) async-start(bf16[8,4,32,2,256]{4,3,2,1,0:T(2,128)(2,1)} %broadcast_in_dim.7), calls=%async_computation | async-start | bytes 2097152 | tf_op jit(solution)/shard_map/all_to_all | solution.py:9
  14.7 26.7 %collective-permute-start.2 = (f32[2,448,2,128]{3,1,2,0:T(8,128)}, f32[2,448,2,128]{3,1,2,0:T(8,128)}, u32[]{:S(2)}, u32[]{:S(2)}) collective-permute-start(f32[2,448,2,128]{3,1,2,0:T(8,128)} %copy.45), channel_id=1, source_target_pairs={{1,0},{2,1},{3,2},{4,3},{5,4},{6,5},{7,6},{8,7},{9,8},{10,9},{11,1... | collective-permute-start | bytes 2752520 | tf_op jit(solution)/shard_map/ppermute | solution.py:31
  18.6 25.4 %collective-permute-start.1 = (f32[2,448,2,128]{3,1,2,0:T(8,128)}, f32[2,448,2,128]{3,1,2,0:T(8,128)}, u32[]{:S(2)}, u32[]{:S(2)}) collective-permute-start(f32[2,448,2,128]{3,1,2,0:T(8,128)} %copy.44), channel_id=1, source_target_pairs={{0,1},{1,2},{2,3},{3,4},{4,5},{5,6},{6,7},{7,8},{8,9},{9,10},{10,1... | collective-permute-start | bytes 2752520 | tf_op jit(solution)/shard_map/ppermute | solution.py:30
  30.0 6.2 copy-start.9
  30.0 6.8 copy-start.8
  57.0 9.8 %collective-permute-start = (bf16[1,256,2,256]{1,3,2,0:T(8,128)(2,1)}, bf16[1,256,2,256]{1,3,2,0:T(8,128)(2,1)S(1)}, u32[]{:S(2)}, u32[]{:S(2)}) collective-permute-start(bf16[1,256,2,256]{1,3,2,0:T(8,128)(2,1)} %get-tuple-element.578), channel_id=1, source_target_pairs={{64,0},{128,64},{192,128},{256,192},{320,256},{384,320},{448,384},... | collective-permute-start | bytes 786440 | tf_op jit(solution)/shard_map/while/body/eval_jaxpr/ppermute | solution.py:47
  68.2 8.6 %collective-permute-start = (bf16[1,256,2,256]{1,3,2,0:T(8,128)(2,1)}, bf16[1,256,2,256]{1,3,2,0:T(8,128)(2,1)S(1)}, u32[]{:S(2)}, u32[]{:S(2)}) collective-permute-start(bf16[1,256,2,256]{1,3,2,0:T(8,128)(2,1)} %get-tuple-element.578), channel_id=1, source_target_pairs={{64,0},{128,64},{192,128},{256,192},{320,256},{384,320},{448,384},... | collective-permute-start | bytes 786440 | tf_op jit(solution)/shard_map/while/body/eval_jaxpr/ppermute | solution.py:47
  78.3 7.7 %collective-permute-start = (bf16[1,256,2,256]{1,3,2,0:T(8,128)(2,1)}, bf16[1,256,2,256]{1,3,2,0:T(8,128)(2,1)S(1)}, u32[]{:S(2)}, u32[]{:S(2)}) collective-permute-start(bf16[1,256,2,256]{1,3,2,0:T(8,128)(2,1)} %get-tuple-element.578), channel_id=1, source_target_pairs={{64,0},{128,64},{192,128},{256,192},{320,256},{384,320},{448,384},... | collective-permute-start | bytes 786440 | tf_op jit(solution)/shard_map/while/body/eval_jaxpr/ppermute | solution.py:47
  87.4 9.1 %collective-permute-start = (bf16[1,256,2,256]{1,3,2,0:T(8,128)(2,1)}, bf16[1,256,2,256]{1,3,2,0:T(8,128)(2,1)S(1)}, u32[]{:S(2)}, u32[]{:S(2)}) collective-permute-start(bf16[1,256,2,256]{1,3,2,0:T(8,128)(2,1)} %get-tuple-element.578), channel_id=1, source_target_pairs={{64,0},{128,64},{192,128},{256,192},{320,256},{384,320},{448,384},... | collective-permute-start | bytes 786440 | tf_op jit(solution)/shard_map/while/body/eval_jaxpr/ppermute | solution.py:47
  98.0 7.6 %collective-permute-start = (bf16[1,256,2,256]{1,3,2,0:T(8,128)(2,1)}, bf16[1,256,2,256]{1,3,2,0:T(8,128)(2,1)S(1)}, u32[]{:S(2)}, u32[]{:S(2)}) collective-permute-start(bf16[1,256,2,256]{1,3,2,0:T(8,128)(2,1)} %get-tuple-element.578), channel_id=1, source_target_pairs={{64,0},{128,64},{192,128},{256,192},{320,256},{384,320},{448,384},... | collective-permute-start | bytes 786440 | tf_op jit(solution)/shard_map/while/body/eval_jaxpr/ppermute | solution.py:47
  107.1 8.2 %collective-permute-start = (bf16[1,256,2,256]{1,3,2,0:T(8,128)(2,1)}, bf16[1,256,2,256]{1,3,2,0:T(8,128)(2,1)S(1)}, u32[]{:S(2)}, u32[]{:S(2)}) collective-permute-start(bf16[1,256,2,256]{1,3,2,0:T(8,128)(2,1)} %get-tuple-element.578), channel_id=1, source_target_pairs={{64,0},{128,64},{192,128},{256,192},{320,256},{384,320},{448,384},... | collective-permute-start | bytes 786440 | tf_op jit(solution)/shard_map/while/body/eval_jaxpr/ppermute | solution.py:47
  116.8 297.7 %collective-permute-start = (bf16[1,256,2,256]{1,3,2,0:T(8,128)(2,1)}, bf16[1,256,2,256]{1,3,2,0:T(8,128)(2,1)S(1)}, u32[]{:S(2)}, u32[]{:S(2)}) collective-permute-start(bf16[1,256,2,256]{1,3,2,0:T(8,128)(2,1)} %get-tuple-element.578), channel_id=1, source_target_pairs={{64,0},{128,64},{192,128},{256,192},{320,256},{384,320},{448,384},... | collective-permute-start | bytes 786440 | tf_op jit(solution)/shard_map/while/body/eval_jaxpr/ppermute | solution.py:47
  429.4 1.1 copy-start.2
  429.6 2.7 copy-start.3
  433.1 2.2 copy-start.1
  435.5 1.0 copy-start.4
  446.7 1.8 copy-start.6
  458.7 14.6 %collective-permute-start = (bf16[1,256,2,256]{1,3,2,0:T(8,128)(2,1)}, bf16[1,256,2,256]{1,3,2,0:T(8,128)(2,1)S(1)}, u32[]{:S(2)}, u32[]{:S(2)}) collective-permute-start(bf16[1,256,2,256]{1,3,2,0:T(8,128)(2,1)} %get-tuple-element.578), channel_id=1, source_target_pairs={{64,0},{128,64},{192,128},{256,192},{320,256},{384,320},{448,384},... | collective-permute-start | bytes 786440 | tf_op jit(solution)/shard_map/while/body/eval_jaxpr/ppermute | solution.py:47
  488.2 1.1 copy-start.2
  488.4 2.7 copy-start.3
  491.9 2.2 copy-start.1
  494.3 1.0 copy-start.4
  506.1 1.8 copy-start.6
  518.7 7.3 %collective-permute-start = (bf16[1,256,2,256]{1,3,2,0:T(8,128)(2,1)}, bf16[1,256,2,256]{1,3,2,0:T(8,128)(2,1)S(1)}, u32[]{:S(2)}, u32[]{:S(2)}) collective-permute-start(bf16[1,256,2,256]{1,3,2,0:T(8,128)(2,1)} %get-tuple-element.578), channel_id=1, source_target_pairs={{64,0},{128,64},{192,128},{256,192},{320,256},{384,320},{448,384},... | collective-permute-start | bytes 786440 | tf_op jit(solution)/shard_map/while/body/eval_jaxpr/ppermute | solution.py:47
  527.5 7.3 %collective-permute-start = (bf16[1,256,2,256]{1,3,2,0:T(8,128)(2,1)}, bf16[1,256,2,256]{1,3,2,0:T(8,128)(2,1)S(1)}, u32[]{:S(2)}, u32[]{:S(2)}) collective-permute-start(bf16[1,256,2,256]{1,3,2,0:T(8,128)(2,1)} %get-tuple-element.578), channel_id=1, source_target_pairs={{64,0},{128,64},{192,128},{256,192},{320,256},{384,320},{448,384},... | collective-permute-start | bytes 786440 | tf_op jit(solution)/shard_map/while/body/eval_jaxpr/ppermute | solution.py:47
  536.2 7.3 %collective-permute-start = (bf16[1,256,2,256]{1,3,2,0:T(8,128)(2,1)}, bf16[1,256,2,256]{1,3,2,0:T(8,128)(2,1)S(1)}, u32[]{:S(2)}, u32[]{:S(2)}) collective-permute-start(bf16[1,256,2,256]{1,3,2,0:T(8,128)(2,1)} %get-tuple-element.578), channel_id=1, source_target_pairs={{64,0},{128,64},{192,128},{256,192},{320,256},{384,320},{448,384},... | collective-permute-start | bytes 786440 | tf_op jit(solution)/shard_map/while/body/eval_jaxpr/ppermute | solution.py:47
  554.0 125.5 %copy-start.5 = (f32[2,448,2,512]{3,2,1,0:T(2,128)S(1)}, f32[2,448,2,512]{3,2,1,0:T(2,128)}, u32[]{:S(2)}) copy-start(f32[2,448,2,512]{3,2,1,0:T(2,128)} %copy.40) | copy-start | bytes 11010052
  554.7 124.8 %slice-start = ((f32[2,448,2,512]{3,2,1,0:T(2,128)}), f32[2,448,2,256]{3,2,1,0:T(2,128)S(1)}, s32[]{:S(2)}) async-start(f32[2,448,2,512]{3,2,1,0:T(2,128)} %copy.40), calls=%async_computation.1 | async-start | bytes 3670016 | tf_op jit(solution)/shard_map/slice | solution.py:180
  554.7 124.8 %collective-permute-start.3 = (bf16[2,448,2,128]{3,2,1,0:T(2,128)(2,1)S(1)}, bf16[2,448,2,128]{3,2,1,0:T(2,128)(2,1)S(1)}, u32[]{:S(2)}, u32[]{:S(2)}) collective-permute-start(bf16[2,448,2,128]{3,2,1,0:T(2,128)(2,1)S(1)} %get-tuple-element.495), channel_id=1, source_target_pairs={{0,1},{1,2},{2,3},{3,4},{4,5},{5,6},{6,7},{7,8},{8,9},{9,10},{10,1... | collective-permute-start | bytes 1376264 | tf_op jit(solution)/shard_map/ppermute | solution.py:53
  674.1 9.8 %collective-permute-start.4 = (bf16[2,448,2,128]{3,2,1,0:T(2,128)(2,1)S(1)}, bf16[2,448,2,128]{3,2,1,0:T(2,128)(2,1)S(1)}, u32[]{:S(2)}, u32[]{:S(2)}) collective-permute-start(bf16[2,448,2,128]{3,2,1,0:T(2,128)(2,1)S(1)} %get-tuple-element.494), channel_id=1, source_target_pairs={{0,63},{1,0},{2,1},{3,2},{4,3},{5,4},{6,5},{7,6},{8,7},{9,8},{10,9... | collective-permute-start | bytes 1376264 | tf_op jit(solution)/shard_map/ppermute | solution.py:53
where the time goes:
time: 689 us; the launch traced here: 686 us
  waiting for transfers between devices  378 us (55%)
  starting transfers between devices  151 us (22%)
  local copies, waits for them, and re-layouts  109 us (16%)
  other arithmetic  20.8 us (3%)
  loops' own time  17.3 us (3%)
  matrix products  9.82 us (1%)
    ppermute x11, waiting for transfers between devices, shifted(): return lax.ppermute(block, axis, route)  371 us
    ppermute x2, starting transfers between devices, passed_along(): return lax.ppermute(value, axis, pairs)  121 us
    dynamic_update_slice x4, local copies, waits for them, and re-layouts, run_block(): lax.dynamic_update_slice(layer_acc, region + term, (row_start, 0, col_sta...  34.8 us
    while x3, local copies, waits for them, and re-layouts, on_device(): lax.fori_loop(0, turn_count, relay_turn, (start_acc, start_waves))  15.4 us
    ppermute x11, starting transfers between devices, shifted(): return lax.ppermute(block, axis, route)  14.1 us
  transfers between devices with their start and end apart: 16, of which 13 were waited for; matrix products, arithmetic and copies ran while one was open for 5% of the time, Pallas kernels for 0%

commit v1 on v0

v1 whole, which is shorter than its diff:
```python
import functools

import jax
import jax.numpy as jnp
from jax import lax
from jax.experimental import pallas as pl
from jax.experimental.pallas import tpu as pltpu
from jax.sharding import PartitionSpec as P

MESH = pl.DeviceIdType.MESH
F32 = jnp.float32
BF16 = jnp.bfloat16

NEED = (96, 160, 224, 256)
FIRST = (80, 144, 208, 256)
SECOND = (64, 128, 192, 256)
PIECE = 32
PAD = 16
BAND = 128
TALL = 80
ROW_STEP = 64


def kernel(
    groups,
    tiles,
    pos_ref,
    cnt_ref,
    taps_ref,
    exit_ref,
    obj_ref,
    st_hbm,
    out_ref,
    waves,
    sends,
    exits,
    ext,
    win,
    back,
    acc,
    place,
    flat,
    inter,
    stored,
    mixer,
    tall,
    mixed,
    rim_send,
    rim_recv,
    grad_send,
    grad_recv,
    recv_sem,
    send_sem,
    exit_sem,
    rim_send_sem,
    rim_recv_sem,
    grad_send_sem,
    grad_recv_sem,
    st_sem,
):
    g = lax.axis_index("depth")
    t = lax.axis_index("tile")
    last = groups - 1
    side = mixer.shape[0] // 2
    slots = waves.shape[0]
    rows = ext.shape[3]
    right = lax.rem(t + 1, tiles)
    left = lax.rem(t + tiles - 1, tiles)

    barrier = pltpu.get_barrier_semaphore()

    def greet(group, tile):
        pl.semaphore_signal(barrier, inc=1, device_id=(group, tile), device_id_type=MESH)

    greet(g, right)
    greet(g, left)

    @pl.when(g == last)
    def _():
        for other in range(last):
            greet(other, t)

    @pl.when(g < last)
    def _():
        greet(last, t)

    @pl.when(g < last - 1)
    def _():
        greet(g + 1, t)

    @pl.when((g > 0) & (g < last))
    def _():
        greet(g - 1, t)

    st_copy = pltpu.make_async_copy(st_hbm, stored, st_sem)
    st_copy.start()

    own_rows = exits.shape[1]
    flat[: slots * own_rows * 4, :] = exit_ref[...].astype(F32)
    for s in range(slots):
        for part in range(2):
            for half in range(2):
                lane = part * side + half * 128
                exits[s, :, lane : lane + 128] = flat[
                    pl.ds(s * own_rows * 4 + half * 2 + part, own_rows, stride=4), :
                ].astype(BF16)

    def spread(layer):
        for part in range(2):
            for half in range(2):
                plane = obj_ref[pl.ds(layer * rows * 4 + half * 2 + part, rows, stride=4), :]
                ext[layer, part, 1 + half] = plane
                rim_send[half, layer, part] = plane.astype(BF16)

    spread(1)

    @pl.when((g == 0) | (g == last - 1))
    def _():
        pl.semaphore_wait(barrier, 4)

    @pl.when((g > 0) & (g < last - 1))
    def _():
        pl.semaphore_wait(barrier, 5)

    @pl.when(g == last)
    def _():
        pl.semaphore_wait(barrier, last + 2)

    def exit_copy(s):
        return pltpu.make_async_remote_copy(
            src_ref=exits.at[s],
            dst_ref=waves.at[s, pl.ds(pl.multiple_of(g * PIECE, PIECE), PIECE), :],
            send_sem=exit_sem.at[s],
            recv_sem=recv_sem.at[s, g],
            device_id=(last, t),
            device_id_type=MESH,
        )

    def own_exit(s):
        return pltpu.make_async_copy(
            exits.at[s],
            waves.at[s, pl.ds(last * PIECE, PIECE), :],
            recv_sem.at[s, last],
        )

    @pl.when(g < last)
    def _():
        for s in range(slots):
            exit_copy(s).start()

    @pl.when(g == last)
    def _():
        for s in range(slots):
            own_exit(s).start()

    def rim_copy(half, layer):
        return pltpu.make_async_remote_copy(
            src_ref=rim_send.at[half, layer],
            dst_ref=rim_recv.at[half, layer],
            send_sem=rim_send_sem.at[half, layer],
            recv_sem=rim_recv_sem.at[half, layer],
            device_id=(g, left if half == 0 else right),
            device_id_type=MESH,
        )

    def grad_copy(half, layer):
        return pltpu.make_async_remote_copy(
            src_ref=grad_send.at[half, layer],
            dst_ref=grad_recv.at[half, layer],
            send_sem=grad_send_sem.at[half, layer],
            recv_sem=grad_recv_sem.at[half, layer],
            device_id=(g, left if half == 0 else right),
            device_id_type=MESH,
        )

    rim_copy(0, 1).start()
    rim_copy(1, 1).start()
    spread(0)
    rim_copy(0, 0).start()
    rim_copy(1, 0).start()

    def mixer_rows(i, carry):
        start = pl.multiple_of(i * 32, 32)
        row = lax.broadcasted_iota(jnp.int32, (32, side), 0) + start
        column = lax.broadcasted_iota(jnp.int32, (32, side), 1)
        tap = column - row + 15
        real = jnp.zeros((32, side), F32)
        imag = jnp.zeros((32, side), F32)
        for k in range(31):
            hit = tap == k
            real = jnp.where(hit, taps_ref[2, k], real)
            imag = jnp.where(hit, taps_ref[3, k], imag)
        real = real.astype(BF16)
        imag = imag.astype(BF16)
        mixer[pl.ds(start, 32), :side] = real
        mixer[pl.ds(start, 32), side:] = -imag
        mixer[pl.ds(side + start, 32), :side] = imag
        mixer[pl.ds(side + start, 32), side:] = real
        return carry

    lax.fori_loop(0, side // 32, mixer_rows, 0)

    row = lax.broadcasted_iota(jnp.int32, (TALL, BAND), 0)
    column = lax.broadcasted_iota(jnp.int32, (TALL, BAND), 1)
    tap = row - column + 15 + PAD
    real = jnp.zeros((TALL, BAND), F32)
    imag = jnp.zeros((TALL, BAND), F32)
    for k in range(31):
        hit = tap == k
        real = jnp.where(hit, taps_ref[0, k], real)
        imag = jnp.where(hit, taps_ref[1, k], imag)
    tall[0, :, :BAND] = real.astype(BF16)
    tall[0, :, BAND:] = imag.astype(BF16)
    tall[1, :, :BAND] = -imag.astype(BF16)
    tall[1, :, BAND:] = real.astype(BF16)

    mixed[...] = jnp.zeros(mixed.shape, BF16)

    first_slot = t * slots

    def windows(s, layer):
        row_start = pos_ref[0, first_slot + s]
        shift = lax.rem(512 - pos_ref[1, first_slot + s], 512)

        def some(i, carry):
            begin = pl.multiple_of(i * ROW_STEP, ROW_STEP)
            for part in range(2):
                blocks = [ext[layer, part, c, pl.ds(row_start + begin, ROW_STEP), :] for c in range(4)]
                turned = pltpu.roll(jnp.concatenate(blocks, axis=1), shift, 1)
                win[layer, s, part, pl.ds(begin, ROW_STEP), :] = turned[:, :side]
            return carry

        lax.fori_loop(0, side // ROW_STEP, some, 0)

    def rim_arrived(layer):
        rim_copy(0, layer).wait_recv()
        rim_copy(1, layer).wait_recv()
        ext[layer, :, 3] = rim_recv[0, layer].astype(F32)
        ext[layer, :, 0] = rim_recv[1, layer].astype(F32)

    rim_arrived(1)
    windows(0, 1)
    rim_arrived(0)
    windows(0, 0)

    @pl.when(g < last)
    def _():
        def some(s, carry):
            windows(s, 1)
            windows(s, 0)
            return carry

        lax.fori_loop(1, slots, some, 0)

    place[...] = jnp.zeros(place.shape, F32)
    acc[...] = jnp.zeros(acc.shape, F32)
    st_copy.wait()

    def piece_copy(s, j):
        span = pl.ds(j * PIECE, PIECE)
        return pltpu.make_async_remote_copy(
            src_ref=sends.at[s, span, :],
            dst_ref=waves.at[s, span, :],
            send_sem=send_sem.at[s, j],
            recv_sem=recv_sem.at[s, j],
            device_id=(g - 1, t),
            device_id_type=MESH,
        )

    def mix(layer, wave, begin):
        v = jnp.dot(wave, mixer[...], preferred_element_type=F32).astype(BF16)
        n = wave.shape[0]
        mixed[layer, 0, PAD + begin : PAD + begin + n, :] = v[:, :side]
        mixed[layer, 1, PAD + begin : PAD + begin + n, :] = v[:, side:]

    def leave(s, layer, begin, end):
        n = end - begin
        lhs = jnp.concatenate([tall[0, :n, :], tall[1, :n, :]], axis=0)
        rhs = jnp.concatenate(
            [mixed[layer, 0, begin : begin + BAND, :], mixed[layer, 1, begin : begin + BAND, :]], axis=0
        )
        h = jnp.dot(lhs, rhs, preferred_element_type=F32)
        real = h[:n]
        imag = h[n:]
        back[layer, 0, begin:end, :] = real
        back[layer, 1, begin:end, :] = imag
        obj_real = win[layer, s, 0, begin:end, :]
        obj_imag = win[layer, s, 1, begin:end, :]
        return jnp.concatenate(
            [obj_real * real + obj_imag * imag, obj_real * imag - obj_imag * real], axis=1
        ).astype(BF16)

    def relay(s):
        came = first_end = second_end = 0
        for step in range(4):
            for j in range(came // PIECE, NEED[step] // PIECE):
                piece_copy(s, j).wait_recv()
            mix(1, waves[s, came : NEED[step], :], came)
            wave = leave(s, 1, first_end, FIRST[step])
            mix(0, wave, first_end)
            sends[s, second_end : SECOND[step], :] = leave(s, 0, second_end, SECOND[step])

            @pl.when(g > 0)
            def _():
                for j in range(second_end // PIECE, SECOND[step] // PIECE):
                    piece_copy(s, j).start()

            came, first_end, second_end = NEED[step], FIRST[step], SECOND[step]

    def gather_grad(s, layer):
        row_start = pos_ref[0, first_slot + s]
        shift = pos_ref[1, first_slot + s]
        live = s < cnt_ref[t]
        begin = pl.multiple_of((layer * slots + s) * side * 4, side * 4)
        flat[...] = stored[pl.ds(begin, side * 4), :].astype(F32)

        def some(i, carry):
            at = pl.multiple_of(i * ROW_STEP, ROW_STEP)
            planes = [flat[pl.ds(at * 4 + q, ROW_STEP, stride=4), :] for q in range(4)]
            st_real = jnp.concatenate([planes[0], planes[2]], axis=1)
            st_imag = jnp.concatenate([planes[1], planes[3]], axis=1)
            real = back[layer, 0, pl.ds(at, ROW_STEP), :]
            imag = back[layer, 1, pl.ds(at, ROW_STEP), :]
            terms = (st_real * real + st_imag * imag, st_real * imag - st_imag * real)
            for part in range(2):
                term = jnp.where(live, terms[part], 0.0)
                wide = jnp.concatenate([term, jnp.zeros((ROW_STEP, side), F32)], axis=1)
                wide = pltpu.roll(wide, shift, 1)
                for c in range(4):
                    place[part, c, pl.ds(rows - side + at, ROW_STEP), :] = wide[:, c * 128 : c * 128 + 128]
            return carry

        lax.fori_loop(0, side // ROW_STEP, some, 0)

        def add(i, carry):
            at = pl.multiple_of(i * ROW_STEP, ROW_STEP)
            for part in range(2):
                for c in range(4):
                    acc[layer, part, c, pl.ds(at, ROW_STEP), :] += place[
                        part, c, pl.ds(rows - side - row_start + at, ROW_STEP), :
                    ]
            return carry

        lax.fori_loop(0, rows // ROW_STEP, add, 0)

    def send_grad(layer):
        grad_send[0, layer] = acc[layer, :, 0].astype(BF16)
        grad_send[1, layer] = acc[layer, :, 3].astype(BF16)
        grad_copy(0, layer).start()
        grad_copy(1, layer).start()

    def turn(s, carry):
        relay(s)

        @pl.when((g == last) & (s < slots - 1))
        def _():
            windows(s + 1, 1)
            windows(s + 1, 0)

        gather_grad(s, 1)

        @pl.when(s == slots - 1)
        def _():
            send_grad(1)

        gather_grad(s, 0)
        return carry

    lax.fori_loop(0, slots, turn, 0)
    send_grad(0)

    for layer in (1, 0):
        grad_copy(0, layer).wait_recv()
        grad_copy(1, layer).wait_recv()
        for part in range(2):
            first = acc[layer, part, 1] + grad_recv[1, layer, part].astype(F32)
            second = acc[layer, part, 2] + grad_recv[0, layer, part].astype(F32)
            inter[pl.ds(part, rows, stride=4), :] = first
            inter[pl.ds(2 + part, rows, stride=4), :] = second
        out_ref[layer * rows * 4 : (layer + 1) * rows * 4, :] = inter[...].astype(BF16)

    @pl.when(g > 0)
    def _():
        def some(s, carry):
            for j in range(side // PIECE):
                piece_copy(s, j).wait_send()
            return carry

        lax.fori_loop(0, slots, some, 0)

    @pl.when(g < last)
    def _():
        for s in range(slots):
            exit_copy(s).wait_send()

    for layer in range(2):
        for half in range(2):
            rim_copy(half, layer).wait_send()
            grad_copy(half, layer).wait_send()


def on_device(exit_grad, stored_waves, object_slices, propagator_taps, positions, counts):
    groups = lax.axis_size("depth")
    tiles = lax.axis_size("tile")
    layers, slots, side = stored_waves.shape[:3]
    own_rows = exit_grad.shape[1]
    rows = object_slices.shape[1]
    lines = layers * rows * 4
    flat_exit = exit_grad.reshape(slots, own_rows, 2, 2, 128).swapaxes(2, 3).reshape(slots * own_rows * 4, 128)
    flat_stored = (
        stored_waves.reshape(layers, slots, side, 2, 2, 128).swapaxes(3, 4).reshape(layers * slots * side * 4, 128)
    )
    flat_object = object_slices.reshape(layers, rows, 2, 2, 128).swapaxes(2, 3).reshape(lines, 128)
    vmem = pl.BlockSpec(memory_space=pltpu.VMEM)
    smem = pl.BlockSpec(memory_space=pltpu.SMEM)
    dma = pltpu.SemaphoreType.DMA
    out = pl.pallas_call(
        functools.partial(kernel, groups, tiles),
        out_shape=jax.ShapeDtypeStruct((lines, 128), BF16),
        in_specs=[smem, smem, smem, vmem, vmem, pl.BlockSpec(memory_space=pl.ANY)],
        out_specs=vmem,
        scratch_shapes=[
            pltpu.VMEM((slots, side, 2 * side), BF16),
            pltpu.VMEM((slots, side, 2 * side), BF16),
            pltpu.VMEM((slots, own_rows, 2 * side), BF16),
            pltpu.VMEM((layers, 2, 4, rows, 128), F32),
            pltpu.VMEM((layers, slots, 2, side, side), F32),
            pltpu.VMEM((layers, 2, side, side), F32),
            pltpu.VMEM((layers, 2, 4, rows, 128), F32),
            pltpu.VMEM((2, 4, 2 * rows - side, 128), F32),
            pltpu.VMEM((side * 4, 128), F32),
            pltpu.VMEM((rows * 4, 128), F32),
            pltpu.VMEM((layers * slots * side * 4, 128), BF16),
            pltpu.VMEM((2 * side, 2 * side), BF16),
            pltpu.VMEM((2, TALL, 2 * BAND), BF16),
            pltpu.VMEM((layers, 2, 336, side), BF16),
            pltpu.VMEM((2, layers, 2, rows, 128), BF16),
            pltpu.VMEM((2, layers, 2, rows, 128), BF16),
            pltpu.VMEM((2, layers, 2, rows, 128), BF16),
            pltpu.VMEM((2, layers, 2, rows, 128), BF16),
            dma((slots, 8)),
            dma((slots, 8)),
            dma((slots,)),
            dma((2, layers)),
            dma((2, layers)),
            dma((2, layers)),
            dma((2, layers)),
            dma,
        ],
        compiler_params=pltpu.CompilerParams(
            collective_id=0, has_side_effects=True, vmem_limit_bytes=48 * 1024 * 1024
        ),
    )(positions.T, counts, propagator_taps.reshape(4, propagator_taps.shape[2]), flat_exit, flat_object, flat_stored)
    return out.reshape(layers, rows, 2, 2, 128).swapaxes(2, 3).reshape(object_slices.shape)


def solution(mesh):
    return jax.shard_map(
        on_device,
        mesh=mesh,
        in_specs=(
            P("tile", "depth", None, None),
            P("depth", "tile", None, None, None),
            P("depth", None, None, "tile"),
            P(),
            P(),
            P(),
        ),
        out_specs=P("depth", None, None, "tile"),
        check_vma=False,
    )
```

time: 689 us -> 96.9 us (0.14)
  the two profiles are of different devices: /device:TPU:9 before, /device:TPU:31 now
where the time goes in v1:
time: 96.9 us; the launch traced here: 96.6 us
  Pallas kernels  89.7 us (93%)
  local copies, waits for them, and re-layouts  6.94 us (7%)
    pallas_call x1, Pallas kernels, on_device(): pl.pallas_call(functools.partial(kernel, groups, tiles), out_shape=jax.Sh...  89.7 us
    unnamed x13, local copies, waits for them, and re-layouts  6.94 us

profile of v1, /device:TPU:31, one launch (start us, length us, event | category | flops | bytes accessed | tf_op | source)
XLA Modules:
  0.0 96.6 jit_solution(4842856833024897886)
XLA Ops:
  0.0 0.0 copy-start
  0.0 1.6 %copy-done = bf16[2,4,256,2,256]{4,3,2,1,0:T(2,128)(2,1)S(1)} copy-done((bf16[2,4,256,2,256]{4,3,2,1,0:T(2,128)(2,1)S(1)}, bf16[2,4,256,2,256]{4,3,2,1,0:T(2,128)(2,1)}, u32[]{:S(2)}) %copy-start) | copy-done | bytes 2097176
  1.6 0.0 copy-start.1
  1.6 1.5 %copy-done.1 = f32[2,448,2,256]{3,2,1,0:T(2,128)S(1)} copy-done((f32[2,448,2,256]{3,2,1,0:T(2,128)S(1)}, f32[2,448,2,256]{3,2,1,0:T(2,128)}, u32[]{:S(2)}) %copy-start.1) | copy-done | bytes 1835032
  3.1 0.0 copy-start.2
  3.1 0.9 copy-done.2
  4.0 0.0 copy-start.3
  4.0 0.7 copy-done.3
  4.7 0.0 copy-start.4
  4.7 0.7 copy-done.4
  5.4 0.0 copy-start.5
  5.4 0.7 copy-done.5
  6.0 89.7 %shard_map.64 = bf16[3584,128]{1,0:T(8,128)(2,1)S(1)} custom-call(s32[2,256]{1,0:T(2,128)S(1)} %bitcast.26, s32[64]{0:T(128)S(1)} %copy-done.5, f32[4,31]{1,0:T(4,128)S(1)} %bitcast.27, bf16[512,128]{1,0:T(8,128)(2,1)S(1)} %bitcast.25, f32[3584,128]{1,0:T(8,128)S(1)} %bitcast.24, bf16[8192,128]{1,0:T(8,128)(2,1)S(1)} %bitcast.23), custom_call_target="tpu_custom_call" | custom-call | tf_op jit(solution)/shard_map/pallas_call | solution.py:417
  95.7 0.9 copy.12
Async XLA Ops:
  0.0 1.6 %copy-start = (bf16[2,4,256,2,256]{4,3,2,1,0:T(2,128)(2,1)S(1)}, bf16[2,4,256,2,256]{4,3,2,1,0:T(2,128)(2,1)}, u32[]{:S(2)}) copy-start(bf16[2,4,256,2,256]{4,3,2,1,0:T(2,128)(2,1)} %param.7) | copy-start | bytes 6291460
  1.6 1.5 %copy-start.1 = (f32[2,448,2,256]{3,2,1,0:T(2,128)S(1)}, f32[2,448,2,256]{3,2,1,0:T(2,128)}, u32[]{:S(2)}) copy-start(f32[2,448,2,256]{3,2,1,0:T(2,128)} %param.8) | copy-start | bytes 5505028
  3.1 0.9 copy-start.2
  4.0 0.7 copy-start.3
  4.7 0.7 copy-start.4
  5.4 0.7 copy-start.5

commit v2 on v1

v2 whole, which is shorter than its diff:
```python
import functools

import jax
import jax.numpy as jnp
from jax import lax
from jax.experimental import pallas as pl
from jax.experimental.pallas import tpu as pltpu
from jax.sharding import PartitionSpec as P

MESH = pl.DeviceIdType.MESH
F32 = jnp.float32
BF16 = jnp.bfloat16

NEED = (96, 160, 224, 256)
FIRST = (80, 144, 208, 256)
SECOND = (64, 128, 192, 256)
PIECE = 32
EDGE = (0, 64, 128, 192, 256)
SHARE = 32
PAD = 16
BAND = 128
TALL = 80


def kernel(
    groups,
    tiles,
    pos_hbm,
    cnt_hbm,
    taps_hbm,
    exit_hbm,
    obj_hbm,
    st_hbm,
    out_ref,
    pos_ref,
    cnt_ref,
    taps_ref,
    exit_ref,
    obj_ref,
    waves,
    sends,
    exits,
    ext,
    win,
    back,
    acc,
    place,
    flat,
    inter,
    stored,
    mixer,
    tall,
    mixed,
    rim_send,
    rim_recv,
    grad_send,
    grad_recv,
    edge_send,
    edge_recv,
    edge,
    recv_sem,
    send_sem,
    exit_sem,
    rim_send_sem,
    rim_recv_sem,
    grad_send_sem,
    grad_recv_sem,
    exit_recv_sem,
    edge_send_sem,
    edge_recv_sem,
    load_sem,
):
    g = lax.axis_index("depth")
    t = lax.axis_index("tile")
    last = groups - 1
    side = mixer.shape[0] // 2
    slots = waves.shape[0]
    rows = ext.shape[3]
    right = lax.rem(t + 1, tiles)
    left = lax.rem(t + tiles - 1, tiles)

    barrier = pltpu.get_barrier_semaphore()

    def greet(group, tile):
        pl.semaphore_signal(barrier, inc=1, device_id=(group, tile), device_id_type=MESH)

    greet(g, right)
    greet(g, left)

    @pl.when(g == last)
    def _():
        for other in range(last):
            greet(other, t)

    @pl.when(g < last)
    def _():
        greet(last, t)

    @pl.when(g < last - 1)
    def _():
        greet(g + 1, t)

    @pl.when((g > 0) & (g < last))
    def _():
        greet(g - 1, t)

    late, early = pl.ds(0, rows * 4), pl.ds(rows * 4, rows * 4)
    sources = (exit_hbm, obj_hbm.at[early, :], obj_hbm.at[late, :], taps_hbm, pos_hbm, cnt_hbm, st_hbm)
    targets = (exit_ref, obj_ref.at[early, :], obj_ref.at[late, :], taps_ref, pos_ref, cnt_ref, stored)
    loads = [pltpu.make_async_copy(a, b, load_sem.at[k]) for k, (a, b) in enumerate(zip(sources, targets))]
    for load in loads:
        load.start()

    loads[0].wait()
    own_rows = exits.shape[1]
    lines = slots * own_rows * 4
    inter[:lines, :] = exit_ref[...].astype(F32)
    for s in range(slots):
        for part in range(2):
            for half in range(2):
                lane = part * side + half * 128
                exits[s, :, lane : lane + 128] = inter[
                    pl.ds(s * own_rows * 4 + half * 2 + part, own_rows, stride=4), :
                ].astype(BF16)

    def spread(layer):
        for part in range(2):
            for half in range(2):
                plane = obj_ref[pl.ds(layer * rows * 4 + half * 2 + part, rows, stride=4), :]
                ext[layer, part, 1 + half] = plane
                rim_send[half, layer, part] = plane.astype(BF16)

    @pl.when((g == 0) | (g == last - 1))
    def _():
        pl.semaphore_wait(barrier, 4)

    @pl.when((g > 0) & (g < last - 1))
    def _():
        pl.semaphore_wait(barrier, 5)

    @pl.when(g == last)
    def _():
        pl.semaphore_wait(barrier, last + 2)

    def exit_copy(s):
        return pltpu.make_async_remote_copy(
            src_ref=exits.at[s],
            dst_ref=waves.at[s, pl.ds(pl.multiple_of(g * SHARE, SHARE), SHARE), :],
            send_sem=exit_sem.at[s],
            recv_sem=exit_recv_sem.at[s, g],
            device_id=(last, t),
            device_id_type=MESH,
        )

    def own_exit(s):
        return pltpu.make_async_copy(
            exits.at[s],
            waves.at[s, pl.ds(last * SHARE, SHARE), :],
            exit_recv_sem.at[s, last],
        )

    def exit_arrival(s, j):
        return pltpu.make_async_copy(
            exits.at[s],
            waves.at[s, pl.ds(j * SHARE, SHARE), :],
            exit_recv_sem.at[s, j],
        )

    def exit_turn(s):
        @pl.when(g < last)
        def _():
            if s > 0:
                exit_copy(s - 1).wait_send()
            if s < slots:
                exit_copy(s).start()

    exit_turn(0)

    @pl.when(g == last)
    def _():
        for s in range(slots):
            own_exit(s).start()

    def rim_copy(half, layer):
        return pltpu.make_async_remote_copy(
            src_ref=rim_send.at[half, layer],
            dst_ref=rim_recv.at[half, layer],
            send_sem=rim_send_sem.at[half, layer],
            recv_sem=rim_recv_sem.at[half, layer],
            device_id=(g, left if half == 0 else right),
            device_id_type=MESH,
        )

    def grad_copy(half, layer):
        return pltpu.make_async_remote_copy(
            src_ref=grad_send.at[half, layer],
            dst_ref=grad_recv.at[half, layer],
            send_sem=grad_send_sem.at[half, layer],
            recv_sem=grad_recv_sem.at[half, layer],
            device_id=(g, left if half == 0 else right),
            device_id_type=MESH,
        )

    loads[1].wait()
    spread(1)
    rim_copy(0, 1).start()
    rim_copy(1, 1).start()
    exit_turn(1)
    loads[2].wait()
    spread(0)
    rim_copy(0, 0).start()
    rim_copy(1, 0).start()
    loads[3].wait()

    def mixer_rows(i, carry):
        start = pl.multiple_of(i * 32, 32)
        row = lax.broadcasted_iota(jnp.int32, (32, side), 0) + start
        column = lax.broadcasted_iota(jnp.int32, (32, side), 1)
        tap = column - row + 15
        real = jnp.zeros((32, side), F32)
        imag = jnp.zeros((32, side), F32)
        for k in range(31):
            hit = tap == k
            real = jnp.where(hit, taps_ref[2, k], real)
            imag = jnp.where(hit, taps_ref[3, k], imag)
        real = real.astype(BF16)
        imag = imag.astype(BF16)
        mixer[pl.ds(start, 32), :side] = real
        mixer[pl.ds(start, 32), side:] = -imag
        mixer[pl.ds(side + start, 32), :side] = imag
        mixer[pl.ds(side + start, 32), side:] = real
        return carry

    lax.fori_loop(0, side // 32, mixer_rows, 0)

    row = lax.broadcasted_iota(jnp.int32, (TALL, BAND), 0)
    column = lax.broadcasted_iota(jnp.int32, (TALL, BAND), 1)
    tap = row - column + 15 + PAD
    real = jnp.zeros((TALL, BAND), F32)
    imag = jnp.zeros((TALL, BAND), F32)
    for k in range(31):
        hit = tap == k
        real = jnp.where(hit, taps_ref[0, k], real)
        imag = jnp.where(hit, taps_ref[1, k], imag)
    tall[0, :, :BAND] = real.astype(BF16)
    tall[0, :, BAND:] = imag.astype(BF16)
    tall[1, :, :BAND] = -imag.astype(BF16)
    tall[1, :, BAND:] = real.astype(BF16)

    exit_turn(2)
    mixed[...] = jnp.zeros(mixed.shape, BF16)
    place[...] = jnp.zeros(place.shape, F32)
    edge[...] = jnp.zeros(edge.shape, F32)
    acc[...] = jnp.zeros(acc.shape, F32)
    for load in loads[4:]:
        load.wait()
    exit_turn(3)

    def place_of(tile, s):
        slot = tile * slots + s
        column = pos_ref[1, slot]
        block = lax.div(column, 128)
        return pos_ref[0, slot], block, column - block * 128

    def lanes(n):
        return lax.broadcasted_iota(jnp.int32, (n, 128), 1)

    def windows(s, layer, slot):
        row_start, block, turn = place_of(t, slot)
        stay = lanes(side) < 128 - turn
        for part in range(2):
            turned = [
                pltpu.roll(ext[layer, part, block + c, pl.ds(row_start, side), :], lax.rem(128 - turn, 128), 1)
                for c in range(3)
            ]
            for c in range(2):
                win[layer, s, part, :, c * 128 : c * 128 + 128] = jnp.where(stay, turned[c], turned[c + 1])

    def rim_arrived(layer):
        rim_copy(0, layer).wait_recv()
        rim_copy(1, layer).wait_recv()
        ext[layer, :, 3] = rim_recv[0, layer].astype(F32)
        ext[layer, :, 0] = rim_recv[1, layer].astype(F32)

    rim_arrived(1)
    windows(0, 1, 0)
    rim_arrived(0)
    windows(0, 0, 0)

    exit_turn(4)

    def piece_copy(s, j):
        span = pl.ds(j * PIECE, PIECE)
        return pltpu.make_async_remote_copy(
            src_ref=sends.at[s, span, :],
            dst_ref=waves.at[s, span, :],
            send_sem=send_sem.at[s, j],
            recv_sem=recv_sem.at[s, j],
            device_id=(g - 1, t),
            device_id_type=MESH,
        )

    def mix(layer, wave, begin):
        v = jnp.dot(wave, mixer[...], preferred_element_type=F32).astype(BF16)
        n = wave.shape[0]
        mixed[layer, 0, PAD + begin : PAD + begin + n, :] = v[:, :side]
        mixed[layer, 1, PAD + begin : PAD + begin + n, :] = v[:, side:]

    def leave(now, layer, begin, end):
        n = end - begin
        lhs = jnp.concatenate([tall[0, :n, :], tall[1, :n, :]], axis=0)
        rhs = jnp.concatenate(
            [mixed[layer, 0, begin : begin + BAND, :], mixed[layer, 1, begin : begin + BAND, :]], axis=0
        )
        h = jnp.dot(lhs, rhs, preferred_element_type=F32)
        real = h[:n]
        imag = h[n:]
        back[layer, 0, begin:end, :] = real
        back[layer, 1, begin:end, :] = imag
        obj_real = win[layer, now, 0, begin:end, :]
        obj_imag = win[layer, now, 1, begin:end, :]
        return jnp.concatenate(
            [obj_real * real + obj_imag * imag, obj_real * imag - obj_imag * real], axis=1
        ).astype(BF16)

    def terms(s, layer, begin, end, edges):
        n = end - begin
        live = s < cnt_ref[t]
        start = pl.multiple_of((layer * slots + s) * side * 4 + begin * 4, 64)
        flat[layer, : n * 4, :] = stored[pl.ds(start, n * 4), :].astype(F32)
        planes = [flat[layer, pl.ds(q, n, stride=4), :] for q in range(4)]
        _, block, turn = place_of(t, s)
        stay = lanes(n) >= turn
        none = jnp.zeros((n, 128), F32)
        for part in range(2):
            turned = []
            for c in range(2):
                st_real, st_imag = planes[2 * c], planes[2 * c + 1]
                real = back[layer, 0, begin:end, c * 128 : c * 128 + 128]
                imag = back[layer, 1, begin:end, c * 128 : c * 128 + 128]
                if part == 0:
                    term = st_real * real + st_imag * imag
                else:
                    term = st_real * imag - st_imag * real
                turned.append(pltpu.roll(jnp.where(live, term, 0.0), turn, 1))
            three = (
                jnp.where(stay, turned[0], none),
                jnp.where(stay, turned[1], turned[0]),
                jnp.where(stay, none, turned[1]),
            )
            for c in range(3):
                place[layer, part, c, rows - side + begin : rows - side + end, :] = three[c]
            if not edges:
                continue
            lane = (layer * 2 + part) * 128
            edge_send[0, begin:end, lane : lane + 128] = jnp.where(block == 0, three[0], none).astype(BF16)
            edge_send[1, begin:end, lane : lane + 128] = jnp.where(block == 0, none, three[2]).astype(BF16)

    def add_terms(s, layer, columns):
        row_start, block, _ = place_of(t, s)
        for part in range(2):
            for c in columns:
                acc[layer, part, c] += place[
                    layer, part, lax.rem(c + 4 - block, 4), pl.ds(rows - side - row_start, rows), :
                ]

    def edge_copy(half, step):
        span = pl.ds(EDGE[step], EDGE[step + 1] - EDGE[step])
        return pltpu.make_async_remote_copy(
            src_ref=edge_send.at[half, span, :],
            dst_ref=edge_recv.at[half, span, :],
            send_sem=edge_send_sem.at[half, step],
            recv_sem=edge_recv_sem.at[half, step],
            device_id=(g, left if half == 0 else right),
            device_id_type=MESH,
        )

    def send_grad(layer):
        grad_send[0, layer] = acc[layer, :, 0].astype(BF16)
        grad_send[1, layer] = acc[layer, :, 3].astype(BF16)
        grad_copy(0, layer).start()
        grad_copy(1, layer).start()

    def last_terms(step):
        for at in range(EDGE[step], EDGE[step + 1], 64):
            for layer in (1, 0):
                terms(slots - 1, layer, at, at + 64, True)
        edge_copy(0, step).start()
        edge_copy(1, step).start()

    def relay(s, final):
        now = lax.rem(s, 2)
        came = first_end = second_end = 0
        for step in range(len(NEED)):

            @pl.when(g < last)
            def _():
                for j in range(came // PIECE, NEED[step] // PIECE):
                    piece_copy(s, j).wait_recv()

            @pl.when(g == last)
            def _():
                for j in range(pl.cdiv(came, SHARE), pl.cdiv(NEED[step], SHARE)):
                    exit_arrival(s, j).wait()

            mix(1, waves[s, came : NEED[step], :], came)
            if step < 2 and not final:
                windows(1 - now, 1 - step, s + 1)
            wave = leave(now, 1, first_end, FIRST[step])
            mix(0, wave, first_end)
            sends[s, second_end : SECOND[step], :] = leave(now, 0, second_end, SECOND[step])

            @pl.when(g > 0)
            def _():
                for j in range(second_end // PIECE, SECOND[step] // PIECE):
                    piece_copy(s, j).start()

            if final and step == 0:
                send_grad(1)
                send_grad(0)
            if final and step < 2:
                pl.when(g == 0)(functools.partial(last_terms, step))
            came, first_end, second_end = NEED[step], FIRST[step], SECOND[step]

    def turn(s, carry):
        relay(s, False)
        for layer in (1, 0):
            for at in range(0, side, 64):
                terms(s, layer, at, at + 64, False)
            add_terms(s, layer, range(4))
        return carry

    lax.fori_loop(0, slots - 1, turn, 0)
    relay(slots - 1, True)

    @pl.when(g > 0)
    def _():
        last_terms(0)
        last_terms(1)

    last_terms(2)
    last_terms(3)
    for layer in (1, 0):
        add_terms(slots - 1, layer, (1, 2))
        for half in range(2):
            grad_copy(half, layer).wait_recv()
        for part in range(2):
            acc[layer, part, 1] += grad_recv[1, layer, part].astype(F32)
            acc[layer, part, 2] += grad_recv[0, layer, part].astype(F32)

    for step in range(len(EDGE) - 1):
        for half in range(2):
            edge_copy(half, step).wait_recv()
            begin, end = EDGE[step], EDGE[step + 1]
            for k in range(4):
                edge[half, k, rows - side + begin : rows - side + end, :] = edge_recv[
                    half, begin:end, k * 128 : k * 128 + 128
                ].astype(F32)

    left_rows = place_of(left, slots - 1)[0]
    right_rows = place_of(right, slots - 1)[0]
    for layer in (1, 0):
        for part in range(2):
            k = layer * 2 + part
            first = acc[layer, part, 1] + edge[1, k, pl.ds(rows - side - left_rows, rows), :]
            second = acc[layer, part, 2] + edge[0, k, pl.ds(rows - side - right_rows, rows), :]
            inter[pl.ds(part, rows, stride=4), :] = first
            inter[pl.ds(2 + part, rows, stride=4), :] = second
        out_ref[layer * rows * 4 : (layer + 1) * rows * 4, :] = inter[...].astype(BF16)

    @pl.when(g > 0)
    def _():
        def some(s, carry):
            for j in range(side // PIECE):
                piece_copy(s, j).wait_send()
            return carry

        lax.fori_loop(0, slots, some, 0)

    for half in range(2):
        for layer in range(2):
            rim_copy(half, layer).wait_send()
            grad_copy(half, layer).wait_send()
        for step in range(len(EDGE) - 1):
            edge_copy(half, step).wait_send()


def on_device(exit_grad, stored_waves, object_slices, propagator_taps, positions, counts):
    groups = lax.axis_size("depth")
    tiles = lax.axis_size("tile")
    layers, slots, side = stored_waves.shape[:3]
    own_rows = exit_grad.shape[1]
    rows = object_slices.shape[1]
    lines = layers * rows * 4
    flat_exit = exit_grad.reshape(slots, own_rows, 2, 2, 128).swapaxes(2, 3).reshape(slots * own_rows * 4, 128)
    flat_stored = (
        stored_waves.reshape(layers, slots, side, 2, 2, 128).swapaxes(3, 4).reshape(layers * slots * side * 4, 128)
    )
    flat_object = object_slices.reshape(layers, rows, 2, 2, 128).swapaxes(2, 3).reshape(lines, 128)
    vmem = pl.BlockSpec(memory_space=pltpu.VMEM)
    dma = pltpu.SemaphoreType.DMA
    out = pl.pallas_call(
        functools.partial(kernel, groups, tiles),
        out_shape=jax.ShapeDtypeStruct((lines, 128), BF16),
        in_specs=[pl.BlockSpec(memory_space=pltpu.HBM)] * 6,
        out_specs=vmem,
        scratch_shapes=[
            pltpu.SMEM((2, positions.shape[0]), jnp.int32),
            pltpu.SMEM(counts.shape, jnp.int32),
            pltpu.SMEM((4, propagator_taps.shape[2]), F32),
            pltpu.VMEM(flat_exit.shape, BF16),
            pltpu.VMEM(flat_object.shape, F32),
            pltpu.VMEM((slots, side, 2 * side), BF16),
            pltpu.VMEM((slots, side, 2 * side), BF16),
            pltpu.VMEM((slots, own_rows, 2 * side), BF16),
            pltpu.VMEM((layers, 2, 4, rows, 128), F32),
            pltpu.VMEM((layers, 2, 2, side, side), F32),
            pltpu.VMEM((layers, 2, side, side), F32),
            pltpu.VMEM((layers, 2, 4, rows, 128), F32),
            pltpu.VMEM((layers, 2, 4, 2 * rows - side, 128), F32),
            pltpu.VMEM((layers, side * 4, 128), F32),
            pltpu.VMEM((rows * 4, 128), F32),
            pltpu.VMEM((layers * slots * side * 4, 128), BF16),
            pltpu.VMEM((2 * side, 2 * side), BF16),
            pltpu.VMEM((2, TALL, 2 * BAND), BF16),
            pltpu.VMEM((layers, 2, 336, side), BF16),
            pltpu.VMEM((2, layers, 2, rows, 128), BF16),
            pltpu.VMEM((2, layers, 2, rows, 128), BF16),
            pltpu.VMEM((2, layers, 2, rows, 128), BF16),
            pltpu.VMEM((2, layers, 2, rows, 128), BF16),
            pltpu.VMEM((2, side, 2 * layers * 128), BF16),
            pltpu.VMEM((2, side, 2 * layers * 128), BF16),
            pltpu.VMEM((2, 2 * layers, 2 * rows - side, 128), F32),
            dma((slots, side // PIECE)),
            dma((slots, side // PIECE)),
            dma((slots,)),
            dma((2, layers)),
            dma((2, layers)),
            dma((2, layers)),
            dma((2, layers)),
            dma((slots, groups)),
            dma((2, len(EDGE) - 1)),
            dma((2, len(EDGE) - 1)),
            dma((7,)),
        ],
        compiler_params=pltpu.CompilerParams(
            collective_id=0, has_side_effects=True, vmem_limit_bytes=48 * 1024 * 1024
        ),
    )(
        *(
            pltpu.with_memory_space_constraint(x, pltpu.HBM)
            for x in (
                positions.T,
                counts,
                propagator_taps.reshape(4, propagator_taps.shape[2]),
                flat_exit,
                flat_object,
                flat_stored,
            )
        )
    )
    return out.reshape(layers, rows, 2, 2, 128).swapaxes(2, 3).reshape(object_slices.shape)


def solution(mesh):
    return jax.shard_map(
        on_device,
        mesh=mesh,
        in_specs=(
            P("tile", "depth", None, None),
            P("depth", "tile", None, None, None),
            P("depth", None, None, "tile"),
            P(),
            P(),
            P(),
        ),
        out_specs=P("depth", None, None, "tile"),
        check_vma=False,
    )
```

time: 96.9 us -> 88.9 us (0.917)
  local copies, waits for them, and re-layouts: 6.94 us -> 0.93 us
  Pallas kernels: 89.7 us -> 88 us
    unnamed x13 -> x1, local copies, waits for them, and re-layouts: 6.94 us -> 0.93 us
    pallas_call x1, Pallas kernels: 89.7 us -> 88 us  [on_device(): pl.pallas_call(functools.partial(kernel, groups, tiles), out_shape=jax.Sh...]
where the time goes in v2:
time: 88.9 us; the launch traced here: 89 us
  Pallas kernels  88 us (99%)
  local copies, waits for them, and re-layouts  0.93 us (1%)
    pallas_call x1, Pallas kernels, on_device(): pl.pallas_call(functools.partial(kernel, groups, tiles), out_shape=jax.Sh...  88 us

profile of v2, /device:TPU:31, one launch (start us, length us, event | category | flops | bytes accessed | tf_op | source)
XLA Modules:
  0.0 89.0 jit_solution(14180473372991121185)
XLA Ops:
  0.0 88.0 %shard_map.64 = bf16[3584,128]{1,0:T(8,128)(2,1)S(1)} custom-call(s32[2,256]{1,0:T(2,128)} %bitcast.26, s32[64]{0:T(128)} %cnt_hbm.1, f32[4,31]{1,0:T(4,128)} %bitcast.27, bf16[512,128]{1,0:T(8,128)(2,1)} %bitcast.25, f32[3584,128]{1,0:T(8,128)} %bitcast.24, bf16[8192,128]{1,0:T(8,128)(2,1)} %bitcast.23), custom_call_target="tpu_custom_call" | custom-call | tf_op jit(solution)/shard_map/pallas_call | solution.py:502
  88.0 0.9 %copy.12 = bf16[2,448,2,256]{3,2,1,0:T(2,128)(2,1)} copy(bf16[2,448,2,256]{3,2,1,0:T(2,128)(2,1)S(1)} %bitcast.22) | data formatting | bytes 1835008

commit v3 on v2

--- a/solution.py
+++ b/solution.py
@@ -11,9 +11,9 @@
 F32 = jnp.float32
 BF16 = jnp.bfloat16
 
-NEED = (96, 160, 224, 256)
-FIRST = (80, 144, 208, 256)
-SECOND = (64, 128, 192, 256)
+NEED = (96, 128, 160, 192, 224, 256)
+FIRST = (80, 112, 144, 176, 208, 256)
+SECOND = (64, 96, 128, 160, 192, 256)
 PIECE = 32
 EDGE = (0, 64, 128, 192, 256)
 SHARE = 32
@@ -248,7 +248,6 @@
     tall[1, :, BAND:] = real.astype(BF16)
 
     exit_turn(2)
-    mixed[...] = jnp.zeros(mixed.shape, BF16)
     place[...] = jnp.zeros(place.shape, F32)
     edge[...] = jnp.zeros(edge.shape, F32)
     acc[...] = jnp.zeros(acc.shape, F32)
@@ -303,20 +302,23 @@
     def mix(layer, wave, begin):
         v = jnp.dot(wave, mixer[...], preferred_element_type=F32).astype(BF16)
         n = wave.shape[0]
-        mixed[layer, 0, PAD + begin : PAD + begin + n, :] = v[:, :side]
-        mixed[layer, 1, PAD + begin : PAD + begin + n, :] = v[:, side:]
-
-    def leave(now, layer, begin, end):
+        blocks = []
+        for part in range(2):
+            half = v[:, part * side : (part + 1) * side]
+            above = mixed[layer, part] if begin else jnp.zeros((PAD, side), BF16)
+            rest = jnp.zeros((BAND - n - above.shape[0], side), BF16)
+            blocks += [above, half, rest]
+            mixed[layer, part] = half[n - 2 * PAD :]
+        return jnp.concatenate(blocks, axis=0)
+
+    def leave(s, now, layer, begin, end, rhs):
         n = end - begin
         lhs = jnp.concatenate([tall[0, :n, :], tall[1, :n, :]], axis=0)
-        rhs = jnp.concatenate(
-            [mixed[layer, 0, begin : begin + BAND, :], mixed[layer, 1, begin : begin + BAND, :]], axis=0
-        )
         h = jnp.dot(lhs, rhs, preferred_element_type=F32)
         real = h[:n]
         imag = h[n:]
-        back[layer, 0, begin:end, :] = real
-        back[layer, 1, begin:end, :] = imag
+        back[s, layer, 0, begin:end, :] = real
+        back[s, layer, 1, begin:end, :] = imag
         obj_real = win[layer, now, 0, begin:end, :]
         obj_imag = win[layer, now, 1, begin:end, :]
         return jnp.concatenate(
@@ -336,8 +338,8 @@
             turned = []
             for c in range(2):
                 st_real, st_imag = planes[2 * c], planes[2 * c + 1]
-                real = back[layer, 0, begin:end, c * 128 : c * 128 + 128]
-                imag = back[layer, 1, begin:end, c * 128 : c * 128 + 128]
+                real = back[s, layer, 0, begin:end, c * 128 : c * 128 + 128]
+                imag = back[s, layer, 1, begin:end, c * 128 : c * 128 + 128]
                 if part == 0:
                     term = st_real * real + st_imag * imag
                 else:
@@ -388,50 +390,66 @@
         edge_copy(0, step).start()
         edge_copy(1, step).start()
 
-    def relay(s, final):
-        now = lax.rem(s, 2)
-        came = first_end = second_end = 0
-        for step in range(len(NEED)):
-
-            @pl.when(g < last)
-            def _():
-                for j in range(came // PIECE, NEED[step] // PIECE):
-                    piece_copy(s, j).wait_recv()
-
-            @pl.when(g == last)
-            def _():
-                for j in range(pl.cdiv(came, SHARE), pl.cdiv(NEED[step], SHARE)):
-                    exit_arrival(s, j).wait()
-
-            mix(1, waves[s, came : NEED[step], :], came)
-            if step < 2 and not final:
-                windows(1 - now, 1 - step, s + 1)
-            wave = leave(now, 1, first_end, FIRST[step])
-            mix(0, wave, first_end)
-            sends[s, second_end : SECOND[step], :] = leave(now, 0, second_end, SECOND[step])
-
-            @pl.when(g > 0)
-            def _():
-                for j in range(second_end // PIECE, SECOND[step] // PIECE):
-                    piece_copy(s, j).start()
-
-            if final and step == 0:
-                send_grad(1)
-                send_grad(0)
-            if final and step < 2:
-                pl.when(g == 0)(functools.partial(last_terms, step))
-            came, first_end, second_end = NEED[step], FIRST[step], SECOND[step]
-
-    def turn(s, carry):
-        relay(s, False)
+    def send_grads():
+        send_grad(1)
+        send_grad(0)
+
+    def collect(s, carry):
         for layer in (1, 0):
             for at in range(0, side, 64):
                 terms(s, layer, at, at + 64, False)
             add_terms(s, layer, range(4))
         return carry
 
+    def relay(s, final):
+        now = lax.rem(s, 2)
+        came = first_end = second_end = 0
+        for step in range(len(NEED)):
+
+            @pl.when(g < last)
+            def _():
+                for j in range(came // PIECE, NEED[step] // PIECE):
+                    piece_copy(s, j).wait_recv()
+
+            @pl.when(g == last)
+            def _():
+                for j in range(pl.cdiv(came, SHARE), pl.cdiv(NEED[step], SHARE)):
+                    exit_arrival(s, j).wait()
+
+            rhs = mix(1, waves[s, came : NEED[step], :], came)
+            if step < 2 and not final:
+                windows(1 - now, 1 - step, s + 1)
+            wave = leave(s, now, 1, first_end, FIRST[step], rhs)
+            rhs = mix(0, wave, first_end)
+            sends[s, second_end : SECOND[step], :] = leave(s, now, 0, second_end, SECOND[step], rhs)
+
+            @pl.when(g > 0)
+            def _():
+                for j in range(second_end // PIECE, SECOND[step] // PIECE):
+                    piece_copy(s, j).start()
+
+            if final and step == 0:
+                pl.when(g <= 1)(send_grads)
+            if final and step in (0, 2):
+                pl.when(g == 0)(functools.partial(last_terms, step // 2))
+            came, first_end, second_end = NEED[step], FIRST[step], SECOND[step]
+
+    def turn(s, carry):
+        relay(s, False)
+
+        @pl.when(g <= 1)
+        def _():
+            collect(s, 0)
+
+        return carry
+
     lax.fori_loop(0, slots - 1, turn, 0)
     relay(slots - 1, True)
+
+    @pl.when(g > 1)
+    def _():
+        lax.fori_loop(0, slots - 1, collect, 0)
+        send_grads()
 
     @pl.when(g > 0)
     def _():
@@ -515,7 +533,7 @@
             pltpu.VMEM((slots, own_rows, 2 * side), BF16),
             pltpu.VMEM((layers, 2, 4, rows, 128), F32),
             pltpu.VMEM((layers, 2, 2, side, side), F32),
-            pltpu.VMEM((layers, 2, side, side), F32),
+            pltpu.VMEM((slots, layers, 2, side, side), F32),
             pltpu.VMEM((layers, 2, 4, rows, 128), F32),
             pltpu.VMEM((layers, 2, 4, 2 * rows - side, 128), F32),
             pltpu.VMEM((layers, side * 4, 128), F32),
@@ -523,7 +541,7 @@
             pltpu.VMEM((layers * slots * side * 4, 128), BF16),
             pltpu.VMEM((2 * side, 2 * side), BF16),
             pltpu.VMEM((2, TALL, 2 * BAND), BF16),
-            pltpu.VMEM((layers, 2, 336, side), BF16),
+            pltpu.VMEM((layers, 2, 2 * PAD, side), BF16),
             pltpu.VMEM((2, layers, 2, rows, 128), BF16),
             pltpu.VMEM((2, layers, 2, rows, 128), BF16),
             pltpu.VMEM((2, layers, 2, rows, 128), BF16),

time: 88.9 us -> 89.8 us (1.010)
  no operation moved by 1% of the time
where the time goes in v3:
time: 89.8 us; the launch traced here: 89.6 us
  Pallas kernels  88.6 us (99%)
  local copies, waits for them, and re-layouts  0.93 us (1%)
    pallas_call x1, Pallas kernels, on_device(): pl.pallas_call(functools.partial(kernel, groups, tiles), out_shape=jax.Sh...  88.6 us

profile of v3, /device:TPU:31, one launch (start us, length us, event | category | flops | bytes accessed | tf_op | source)
XLA Modules:
  0.0 89.6 jit_solution(16902088202266420927)
XLA Ops:
  0.0 88.6 %shard_map.64 = bf16[3584,128]{1,0:T(8,128)(2,1)S(1)} custom-call(s32[2,256]{1,0:T(2,128)} %bitcast.26, s32[64]{0:T(128)} %cnt_hbm.1, f32[4,31]{1,0:T(4,128)} %bitcast.27, bf16[512,128]{1,0:T(8,128)(2,1)} %bitcast.25, f32[3584,128]{1,0:T(8,128)} %bitcast.24, bf16[8192,128]{1,0:T(8,128)(2,1)} %bitcast.23), custom_call_target="tpu_custom_call" | custom-call | tf_op jit(solution)/shard_map/pallas_call | solution.py:520
  88.7 0.9 %copy.12 = bf16[2,448,2,256]{3,2,1,0:T(2,128)(2,1)} copy(bf16[2,448,2,256]{3,2,1,0:T(2,128)(2,1)S(1)} %bitcast.22) | data formatting | bytes 1835008
